TPU v7x, 32 devices: a whole 2x2x4 slice. The times are simulated.
32 devices in a mesh: samp: 2 (over x), gene: 4 (over z), snp: 4 (over y, core).
Axes of the slice: x: 2, y: 2, z: 4, core: 2. Of those that a mesh axis runs over, the one named last changes fastest.
Arguments:
- expression: bfloat16 [512, 2048], P('samp', ('gene', 'snp')), may hold values from -6 to 6
- loadings: bfloat16 [2048, 128], P(('gene', 'snp')), may hold values from -0.125 to 0.125
- dosage: bfloat16 [512, 16384], P(None, ('gene', 'snp')), may hold values from 0 to 2
Outputs:
- assoc: bfloat16 [16, 2, 64, 16384], P(None, 'samp', None, ('gene', 'snp'))
All inputs are finite; a program needn't handle non-finite values.
Results may differ from a plain program's by a relative error of at most 0.0065.
Values may be sent and summed in bfloat16 or wider, within the bound.
A program may use at most 64 MiB of HBM per device.

v0:
```python
import jax
import jax.numpy as jnp
from jax import lax
from jax.sharding import PartitionSpec as P

ridge_factor = 1.0
ridge_sample = 1.0


def body(expression, loadings, dosage):
    contract = (((0,), (0,)), ((), ()))
    factor_count = loadings.shape[1]
    identity = jnp.eye(factor_count, dtype=jnp.float32)
    panel_genes = expression.shape[1] // lax.axis_size("samp")
    all_samples = dosage.shape[0]
    snp_count = dosage.shape[1]
    block_count = lax.axis_size("gene") * lax.axis_size("snp")
    norm_scale = 1.0 / jnp.sqrt(jnp.float32(all_samples))
    panel_expr = lax.all_to_all(expression.T, "samp", split_axis=0, concat_axis=1, tiled=True)
    local_factor = jnp.dot(expression, loadings, preferred_element_type=jnp.float32)
    local_gram = lax.dot_general(loadings, loadings, contract, preferred_element_type=jnp.float32)
    factor_sum, gram_sum = lax.psum((local_factor, local_gram), ("gene", "snp"))
    lower_gram = jnp.linalg.cholesky(gram_sum + ridge_factor * identity)
    factors = jax.scipy.linalg.cho_solve((lower_gram, True), factor_sum.T).T.astype(jnp.bfloat16)
    local_hess = lax.dot_general(factors, factors, contract, preferred_element_type=jnp.float32)
    local_cross = lax.dot_general(factors, expression, contract, preferred_element_type=jnp.float32)
    hess_sum, cross_sum = lax.psum((local_hess, local_cross), "samp")
    lower_hess = jnp.linalg.cholesky(hess_sum + ridge_sample * identity)
    fit_coef = jax.scipy.linalg.cho_solve((lower_hess, True), cross_sum).astype(jnp.bfloat16)
    all_fac = lax.all_gather(factors, "samp", axis=0, tiled=True)
    own_coef = lax.dynamic_slice_in_dim(
        fit_coef, lax.axis_index("samp") * panel_genes, panel_genes, 1
    )
    coef_rows = lax.all_gather(own_coef.T, ("gene", "snp"), axis=0, tiled=True)
    fitted = lax.dot_general(
        coef_rows, all_fac, (((1,), (1,)), ((), ())), preferred_element_type=jnp.float32
    )
    residual = (
        lax.all_gather(panel_expr, ("gene", "snp"), axis=0, tiled=True).astype(jnp.float32) - fitted
    ).astype(jnp.bfloat16)
    totals = jnp.dot(residual, dosage, preferred_element_type=jnp.float32) * norm_scale
    return totals.astype(jnp.bfloat16).reshape(block_count, 1, panel_genes, snp_count)


def solution(mesh):
    placed = (P("samp", ("gene", "snp")), P(("gene", "snp"), None), P(None, ("gene", "snp")))
    return jax.shard_map(
        body,
        mesh=mesh,
        in_specs=placed,
        out_specs=P(None, "samp", None, ("gene", "snp")),
        check_vma=False,
    )
```

profile of v0, /device:TPU:0, one launch (start us, length us, event | category | flops | bytes accessed | tf_op | source)
XLA Modules:
  0.0 212.4 jit_solution(1605014639610106751)
XLA Ops:
  6.5 0.0 copy-start
  6.5 0.0 copy-start.1
  6.5 0.0 all-reduce.5.cloned.1.call-start
  6.5 1.7 fusion.14
  8.3 1.6 fusion.15
  9.9 0.0 all-reduce.5.cloned.1.call-update
  9.9 0.0 all-reduce.7.cloned.1.call-start
  10.0 93.5 %all-reduce.5.cloned.1.call-done = (f32[256,128]{1,0:T(8,128)}, f32[128,128]{0,1:T(8,128)}) async-done(((f32[256,128]{1,0:T(8,128)}, f32[128,128]{0,1:T(8,128)}), (f32[256,128]{1,0:T(8,128)}, f32[128,128]{0,1:T(8,128)})) %all-reduce.5.cloned.1.call-update) | async-done | bytes 196624 | tf_op jit(solution)/shard_map/psum | solution.py:22
  103.4 0.9 convert_add_fusion.1
  104.3 0.1 copy.19
  104.4 0.9 fusion.10
  105.2 11.7 %cholesky.44 = f32[128,128]{1,0:T(8,128)S(1)} custom-call(f32[128,128]{1,0:T(8,128)S(1)} %fusion.10), custom_call_target="Cholesky" | custom-call | tf_op jit(solution)/shard_map/jit(cholesky)/cholesky | solution.py:23
  117.0 0.6 compare_reduce_fusion.1
  117.6 0.7 fusion
  118.3 9.8 %custom-call.16 = f32[1,128,128]{1,2,0:T(8,128)S(1)} custom-call(f32[1,128,128]{2,1,0:T(8,128)S(1)} %fusion), custom_call_target="InvertDiagBlocksLowerTriangular" | custom-call | tf_op jit(solution)/shard_map/jit(_cho_solve)/triangular_solve | solution.py:24
  128.1 1.2 fusion.8
  129.3 0.4 convolution_convert_fusion
  129.7 1.7 fusion.17
  131.4 0.8 fusion.16
  132.2 0.0 all-reduce.7.cloned.1.call-update
  132.3 0.0 all-gather.2.cloned.1.call-start
  132.3 0.0 copy-done.1
  132.3 0.1 copy.16
  132.4 7.3 %all_to_all.19 = bf16[2,64,256]{2,1,0:T(8,128)(2,1)S(1)} all-to-all(bf16[2,64,256]{2,1,0:T(8,128)(2,1)S(1)} %bitcast.50), channel_id=1, replica_groups=mesh['samp'=2,'gene'=4,'snp'=4] {'samp'}, dimensions={0} | all-to-all | bytes 131072 | tf_op jit(solution)/shard_map/all_to_all | solution.py:19
  139.7 0.6 copy.25
  140.4 0.0 all-gather.2.cloned.1.call-update
  140.4 5.1 %all_gather.11 = bf16[512,128]{1,0:T(8,128)(2,1)S(1)} all-gather(bf16[256,128]{1,0:T(8,128)(2,1)S(1)} %convolution_convert_fusion), channel_id=1, replica_groups=mesh['samp'=2,'gene'=4,'snp'=4] {'samp'}, dimensions={0}, use_global_device_ids=true | all-gather | bytes 196608 | tf_op jit(solution)/shard_map/all_gather | solution.py:30
  145.5 8.1 %all-reduce.7.cloned.1.call-done = (f32[128,128]{1,0:T(8,128)}, f32[128,128]{0,1:T(8,128)}) async-done(((f32[128,128]{1,0:T(8,128)}, f32[128,128]{0,1:T(8,128)}), (f32[128,128]{1,0:T(8,128)}, f32[128,128]{0,1:T(8,128)})) %all-reduce.7.cloned.1.call-update) | async-done | bytes 131088 | tf_op jit(solution)/shard_map/psum | solution.py:27
  153.7 0.9 convert_add_fusion
  154.5 0.1 copy.21
  154.6 0.9 fusion.6
  155.5 11.7 %cholesky.55 = f32[128,128]{1,0:T(8,128)S(1)} custom-call(f32[128,128]{1,0:T(8,128)S(1)} %fusion.6), custom_call_target="Cholesky" | custom-call | tf_op jit(solution)/shard_map/jit(cholesky)/cholesky | solution.py:28
  167.2 0.6 compare_reduce_fusion
  167.8 0.6 fusion.1
  168.4 9.8 %custom-call.17 = f32[1,128,128]{1,2,0:T(8,128)S(1)} custom-call(f32[1,128,128]{2,1,0:T(8,128)S(1)} %fusion.1), custom_call_target="InvertDiagBlocksLowerTriangular" | custom-call | tf_op jit(solution)/shard_map/jit(_cho_solve)/triangular_solve | solution.py:29
  178.2 1.1 fusion.4
  179.4 0.3 fusion.2
  179.7 22.1 %all_gather.10 = bf16[1024,128]{1,0:T(8,128)(2,1)S(1)} all-gather(bf16[64,128]{1,0:T(8,128)(2,1)S(1)} %fusion.13), channel_id=1, replica_groups=mesh['samp'=2,'gene'=4,'snp'=4] {'gene','snp'}, dimensions={0}, use_global_device_ids=true | all-gather | bytes 278528 | tf_op jit(solution)/shard_map/all_gather | solution.py:34
  201.8 0.0 all-gather.2.cloned.1.call-done
  201.8 0.0 copy-done
  201.8 4.1 %multiply_convert_fusion = bf16[1024,1024]{1,0:T(8,128)(2,1)} fusion(bf16[512,1024]{1,0:T(8,128)(2,1)S(1)} %copy-done, bf16[1024,512]{1,0:T(8,128)(2,1)} %all-gather.2.cloned.1.call-done, bf16[1024,128]{1,0:T(8,128)(2,1)S(1)} %all_gather.10, bf16[512,128]{1,0:T(8,128)(2,1)S(1)} %all_gather.11), kind=kOutput, calls=%fused_computation | convolution fusion | flops 1211629568 | bytes 4587520 | tf_op jit(solution)/shard_map/dot_general | solution.py:41
  (3 shorter events, 0.1 us)
Async XLA Ops:
  6.5 195.3 %copy-start = (bf16[512,1024]{1,0:T(8,128)(2,1)S(1)}, bf16[512,1024]{1,0:T(8,128)(2,1)}, u32[]{:S(2)}) copy-start(bf16[512,1024]{1,0:T(8,128)(2,1)} %param.6) | copy-start | bytes 3145732
  6.5 125.8 %copy-start.1 = (bf16[256,128]{1,0:T(8,128)(2,1)S(1)}, bf16[256,128]{1,0:T(8,128)(2,1)}, u32[]{:S(2)}) copy-start(bf16[256,128]{1,0:T(8,128)(2,1)} %param.4) | copy-start | bytes 196612
  6.5 96.9 %all-reduce.5.cloned.1.call-start = ((), (), s32[]{:S(2)}) async-start(), calls=%async_computation.2 | async-start | bytes 393216 | tf_op jit(solution)/shard_map/psum | solution.py:22
  9.9 143.7 %all-reduce.7.cloned.1.call-start = ((), (), s32[]{:S(2)}) async-start(), calls=%async_computation.3 | async-start | bytes 262144 | tf_op jit(solution)/shard_map/psum | solution.py:27
  132.3 69.5 %all-gather.2.cloned.1.call-start = ((), (), s32[]{:S(2)}) async-start(), calls=%async_computation.1 | async-start | bytes 1114112 | tf_op jit(solution)/shard_map/all_gather | solution.py:39
Sparse Core Ops, SparseCore 0:
  10.9 92.4 all-reduce.4
  132.4 21.2 all-reduce.6
  155.8 38.8 all-gather.1
where the time goes:
time: 213 us; the launch traced here: 212 us
  waiting for transfers between devices  102 us (48%)
  other arithmetic  49 us (23%)
  blocking collectives  34.5 us (16%)
  between operations  13.2 us (6%)
  matrix products  12.9 us (6%)
    psum x1, waiting for transfers between devices, body(): factor_sum, gram_sum = lax.psum((local_factor, local_gram), ('gene', 'snp'))  93.5 us
    all_gather x1, blocking collectives, body(): coef_rows = lax.all_gather(own_coef.T, ('gene', 'snp'), axis=0, tiled=True)  22.1 us
    another operation x3, other arithmetic, body(): lower_gram = jnp.linalg.cholesky(gram_sum + ridge_factor * identity)  12.4 us
    another operation x3, other arithmetic, body(): lower_hess = jnp.linalg.cholesky(hess_sum + ridge_sample * identity)  12.4 us
    another operation x2, other arithmetic, body(): jax.scipy.linalg.cho_solve((lower_gram, True), factor_sum.T)  10.5 us
    another operation x2, other arithmetic, body(): jax.scipy.linalg.cho_solve((lower_hess, True), cross_sum)  10.4 us
    psum x1, waiting for transfers between devices, body(): hess_sum, cross_sum = lax.psum((local_hess, local_cross), 'samp')  8.15 us
    all_to_all x1, blocking collectives, body(): lax.all_to_all(expression.T, 'samp', split_axis=0, concat_axis=1, tiled=T...  7.3 us
  transfers between devices with their start and end apart: 3, of which 2 were waited for; matrix products, arithmetic and copies ran while one was open for 13% of the time, Pallas kernels for 0%

commit v1 on v0

v1 whole, which is shorter than its diff:
```python
import functools

import jax
import jax.numpy as jnp
from jax import lax
from jax.experimental import pallas as pl
from jax.experimental.pallas import tpu as pltpu
from jax.sharding import PartitionSpec as P

ridge_factor = 1.0
ridge_sample = 1.0
MESH = pl.DeviceIdType.MESH
VMEM_LIMIT = 56 * 1024 * 1024


def eye(n, value):
    rows = lax.broadcasted_iota(jnp.int32, (n, n), 0)
    cols = lax.broadcasted_iota(jnp.int32, (n, n), 1)
    return jnp.where(rows == cols, jnp.float32(value), jnp.float32(0.0))


def spd_inverse(a):
    n = a.shape[0]
    lane_top = lax.broadcasted_iota(jnp.int32, (8, n), 1)
    sub_top = lax.broadcasted_iota(jnp.int32, (8, n), 0)
    lane_rest = lax.broadcasted_iota(jnp.int32, (n - 8, n), 1)

    def round_of_pivots(_, a):
        top, rest = a[:8], a[8:]
        for k in range(8):
            row = top[k : k + 1, :]
            inv = 1.0 / row[:, k : k + 1]
            scaled = jnp.where(lane_top[:1] == k, inv, row * inv)
            top_col = jnp.where(sub_top == k, -1.0, jnp.broadcast_to(top[:, k : k + 1], (8, n)))
            rest_col = rest[:, k : k + 1]
            top = jnp.where((sub_top == k) | (lane_top == k), 0.0, top) - top_col * scaled
            rest = jnp.where(lane_rest == k, 0.0, rest) - rest_col * scaled
        return pltpu.roll(jnp.concatenate([rest, top], axis=0), n - 8, 1)

    return lax.fori_loop(0, n // 8, round_of_pivots, a)


def halves(x):
    high = x.astype(jnp.bfloat16)
    low = (x - high.astype(jnp.float32)).astype(jnp.bfloat16)
    return high, low


def factor_kernel(
    sizes, expr_ref, load_ref, panel_ref, fac_ref, proj_ref,
    part, got, own, gram_all, sum_all, expr_t,
    rs_send, rs_recv, ag_send, ag_recv, gram_send, gram_recv, x_send, x_recv, pan_send, pan_recv,
):
    ns, ng, np_ = sizes
    nb = ng * np_
    total = ns * nb
    nl = 2 if np_ % 2 == 0 else 1
    nh = np_ // nl
    s_loc = expr_ref.shape[0]
    k = load_ref.shape[1]
    gp = expr_ref.shape[1] // ns
    rows_f, rows_g = s_loc // nb, k // nb
    s, g, p = lax.axis_index("samp"), lax.axis_index("gene"), lax.axis_index("snp")
    b = g * np_ + p
    q = s * nb + b
    hi, lo = p // nl, p % nl

    def place(q_):
        s_, b_ = q_ // nb, q_ % nb
        return (s_, b_ // np_, b_ % np_), s_, b_

    barrier = pltpu.get_barrier_semaphore()

    def greet(j, c):
        dev, _, _ = place(lax.rem(q + j, total))
        pl.semaphore_signal(barrier, inc=1, device_id=dev, device_id_type=MESH)
        return c

    lax.fori_loop(1, total, greet, 0)

    expr = expr_ref[...]
    load = load_ref[...]
    fac_part = jnp.dot(expr, load, preferred_element_type=jnp.float32)
    part[:, :rows_f, :] = fac_part.reshape(nb, rows_f, k)
    gram_part = lax.dot_general(load, load, (((0,), (0,)), ((), ())), preferred_element_type=jnp.float32)
    part[:, rows_f:, :] = gram_part.reshape(nb, rows_g, k)
    expr_t[...] = expr.T

    pl.semaphore_wait(barrier, total - 1)

    def rs_copy(j):
        peer = lax.rem(b + j, nb)
        return pltpu.make_async_remote_copy(
            src_ref=part.at[peer], dst_ref=got.at[j],
            send_sem=rs_send.at[j], recv_sem=rs_recv.at[j],
            device_id=(s, peer // np_, peer % np_), device_id_type=MESH,
        )

    def x_copy(i, arriving=False):
        peer = lax.rem(s + i, ns)
        source = lax.rem(s - i + ns, ns) if arriving else s
        return pltpu.make_async_remote_copy(
            src_ref=expr_t.at[pl.ds(pl.multiple_of(peer * gp, gp), gp), :],
            dst_ref=panel_ref.at[b, :, pl.ds(pl.multiple_of(source * s_loc, s_loc), s_loc)],
            send_sem=x_send.at[i], recv_sem=x_recv.at[i],
            device_id=(peer, g, p), device_id_type=MESH,
        )

    def loop(lo_, hi_, fn):
        def step(i, c):
            fn(i)
            return c

        lax.fori_loop(lo_, hi_, step, 0)

    loop(1, nb, lambda j: rs_copy(j).start())
    loop(1, ns, lambda i: x_copy(i).start())
    panel_ref[b, :, pl.ds(pl.multiple_of(s * s_loc, s_loc), s_loc)] = expr_t[
        pl.ds(pl.multiple_of(s * gp, gp), gp), :
    ]

    loop(1, nb, lambda j: rs_copy(j).wait_recv())
    acc = part[b]
    for j in range(1, nb):
        acc = acc + got[j]
    own[...] = acc

    def gram_copy(j, arriving=False):
        peer = lax.rem(b + j, nb)
        source = lax.rem(b - j + nb, nb) if arriving else b
        return pltpu.make_async_remote_copy(
            src_ref=own.at[pl.ds(rows_f, rows_g), :],
            dst_ref=gram_all.at[pl.ds(pl.multiple_of(source * rows_g, rows_g), rows_g), :],
            send_sem=gram_send.at[j], recv_sem=gram_recv.at[j],
            device_id=(s, peer // np_, peer % np_), device_id_type=MESH,
        )

    def sum_copy(j, arriving=False):
        dev, _, _ = place(lax.rem(q + j, total))
        source = lax.rem(q - j + total, total) if arriving else q
        return pltpu.make_async_remote_copy(
            src_ref=own.at[pl.ds(0, rows_f), :],
            dst_ref=sum_all.at[pl.ds(pl.multiple_of(source * rows_f, rows_f), rows_f), :],
            send_sem=ag_send.at[j], recv_sem=ag_recv.at[j],
            device_id=dev, device_id_type=MESH,
        )

    loop(1, nb, lambda j: gram_copy(j).start())
    loop(1, total, lambda j: sum_copy(j).start())
    gram_all[pl.ds(pl.multiple_of(b * rows_g, rows_g), rows_g), :] = acc[rows_f:]
    sum_all[pl.ds(pl.multiple_of(q * rows_f, rows_f), rows_f), :] = acc[:rows_f]

    def pan_copy(slot, block, dev):
        return pltpu.make_async_remote_copy(
            src_ref=panel_ref.at[block], dst_ref=panel_ref.at[block],
            send_sem=pan_send.at[slot], recv_sem=pan_recv.at[block],
            device_id=dev, device_id_type=MESH,
        )

    def gene_send(i):
        return pan_copy(i, b, (s, lax.rem(g + i, ng), p))

    def high_send(i):
        h, g_ = 1 + i // ng, i % ng
        return pan_copy(ng + i, g_ * np_ + p, (s, g, lax.rem(hi + h, nh) * nl + lo))

    def low_send(i):
        g_, h = i // nh, i % nh
        return pan_copy(
            ng + ng * (nh - 1) + i, g_ * np_ + h * nl + lo, (s, g, hi * nl + lax.rem(lo + 1, nl))
        )

    n_high = ng * (nh - 1)
    n_low = nb // nl if nl > 1 else 0

    loop(1, ns, lambda i: x_copy(i, True).wait_recv())
    loop(1, ng, lambda i: gene_send(i).start())

    loop(1, nb, lambda j: gram_copy(j, True).wait_recv())
    gram_inv = spd_inverse(gram_all[...] + eye(k, ridge_factor))

    me = (s, g, p)
    loop(1, ng, lambda i: pan_copy(0, lax.rem(g + i, ng) * np_ + p, me).wait_recv())
    loop(0, n_high, lambda i: high_send(i).start())

    loop(1, total, lambda j: sum_copy(j, True).wait_recv())
    factors = jnp.dot(
        sum_all[...], gram_inv, preferred_element_type=jnp.float32, precision=lax.Precision.HIGHEST
    ).astype(jnp.bfloat16)
    fac_ref[...] = factors
    hess = lax.dot_general(
        factors, factors, (((0,), (0,)), ((), ())), preferred_element_type=jnp.float32
    )
    hess_inv = spd_inverse(hess + eye(k, ridge_sample))

    def high_wait(i):
        h, g_ = 1 + i // ng, i % ng
        pan_copy(0, g_ * np_ + lax.rem(hi + h, nh) * nl + lo, me).wait_recv()

    loop(0, n_high, high_wait)
    loop(0, n_low, lambda i: low_send(i).start())

    inv_high, inv_low = halves(hess_inv)
    proj = jnp.dot(factors, inv_high, preferred_element_type=jnp.float32) + jnp.dot(
        factors, inv_low, preferred_element_type=jnp.float32
    )
    proj_high, proj_low = halves(proj)
    proj_ref[:, :k] = proj_high
    proj_ref[:, k:] = proj_low

    def low_wait(i):
        g_, h = i // nh, i % nh
        pan_copy(0, g_ * np_ + h * nl + lax.rem(lo + 1, nl), me).wait_recv()

    loop(0, n_low, low_wait)

    loop(1, nb, lambda j: rs_copy(j).wait_send())
    loop(1, ns, lambda i: x_copy(i).wait_send())
    loop(1, nb, lambda j: gram_copy(j).wait_send())
    loop(1, total, lambda j: sum_copy(j).wait_send())
    loop(1, ng, lambda i: gene_send(i).wait_send())
    loop(0, n_high, lambda i: high_send(i).wait_send())
    loop(0, n_low, lambda i: low_send(i).wait_send())


def assoc_kernel(norm_scale, panel_ref, proj_ref, fac_ref, dosage_ref, out_ref):
    panel = panel_ref[...]
    k = fac_ref.shape[1]
    both = jnp.dot(panel, proj_ref[...], preferred_element_type=jnp.float32)
    coef = (both[:, :k] + both[:, k:]).astype(jnp.bfloat16)
    fitted = lax.dot_general(
        coef, fac_ref[...], (((1,), (1,)), ((), ())), preferred_element_type=jnp.float32
    )
    residual = (panel.astype(jnp.float32) - fitted).astype(jnp.bfloat16)
    totals = jnp.dot(residual, dosage_ref[...], preferred_element_type=jnp.float32)
    out_ref[...] = (totals * norm_scale).astype(jnp.bfloat16)


def body(expression, loadings, dosage):
    ns, ng, np_ = lax.axis_size("samp"), lax.axis_size("gene"), lax.axis_size("snp")
    nb = ng * np_
    total = ns * nb
    s_loc, g_loc = expression.shape
    k = loadings.shape[1]
    gp = g_loc // ns
    samples, snps = dosage.shape
    rows_f, rows_g = s_loc // nb, k // nb
    f32, bf16 = jnp.float32, jnp.bfloat16
    dma = pltpu.SemaphoreType.DMA
    vmem = pl.BlockSpec(memory_space=pltpu.VMEM)
    n_pan = ng + np_ * ng + nb
    panels, factors, proj = pl.pallas_call(
        functools.partial(factor_kernel, (ns, ng, np_)),
        out_shape=(
            jax.ShapeDtypeStruct((nb, gp, samples), bf16),
            jax.ShapeDtypeStruct((samples, k), bf16),
            jax.ShapeDtypeStruct((samples, 2 * k), bf16),
        ),
        in_specs=[vmem, vmem],
        out_specs=(vmem, vmem, vmem),
        scratch_shapes=[
            pltpu.VMEM((nb, rows_f + rows_g, k), f32),
            pltpu.VMEM((nb, rows_f + rows_g, k), f32),
            pltpu.VMEM((rows_f + rows_g, k), f32),
            pltpu.VMEM((k, k), f32),
            pltpu.VMEM((samples, k), f32),
            pltpu.VMEM((g_loc, s_loc), bf16),
            dma((nb,)), dma((nb,)), dma((total,)), dma((total,)), dma((nb,)), dma((nb,)),
            dma((ns,)), dma((ns,)), dma((n_pan,)), dma((nb,)),
        ],
        compiler_params=pltpu.CompilerParams(
            collective_id=0, has_side_effects=True, vmem_limit_bytes=VMEM_LIMIT
        ),
        name="factor_exchange",
    )(expression, loadings)
    rows = min(4 * gp, nb * gp)
    const = lambda i: (0, 0)
    out = pl.pallas_call(
        functools.partial(assoc_kernel, 1.0 / samples**0.5),
        grid=(nb * gp // rows,),
        out_shape=jax.ShapeDtypeStruct((nb * gp, snps), bf16),
        in_specs=[
            pl.BlockSpec((rows, samples), lambda i: (i, 0)),
            pl.BlockSpec((samples, 2 * k), const),
            pl.BlockSpec((samples, k), const),
            pl.BlockSpec((samples, snps), const),
        ],
        out_specs=pl.BlockSpec((rows, snps), lambda i: (i, 0)),
        compiler_params=pltpu.CompilerParams(vmem_limit_bytes=VMEM_LIMIT),
        name="association",
    )(panels.reshape(nb * gp, samples), proj, factors, dosage)
    return out.reshape(nb, 1, gp, snps)


def solution(mesh):
    placed = (P("samp", ("gene", "snp")), P(("gene", "snp"), None), P(None, ("gene", "snp")))
    return jax.shard_map(
        body,
        mesh=mesh,
        in_specs=placed,
        out_specs=P(None, "samp", None, ("gene", "snp")),
        check_vma=False,
    )
```

time: 213 us -> 54 us (0.25)
  waiting for transfers between devices: 102 us -> 0 us
  Pallas kernels: 0 us -> 53.8 us
  other arithmetic: 49 us -> 0 us
  blocking collectives: 34.5 us -> 0 us
  between operations: 13.2 us -> 0.01 us
  matrix products: 12.9 us -> 0 us
    psum x2 -> x0, waiting for transfers between devices: 102 us -> none  [the longest x1 93.5 us: body(): factor_sum, gram_sum = lax.psum((local_factor, local_gram), ('gene', 'snp'))]
    pallas_call x0 -> x2, Pallas kernels: none -> 53.8 us  [the longest x1 48 us: body(): pl.pallas_call(functools.partial(factor_kernel, (ns, ng, np_)), out_shape...]
    another operation x10 -> x0, other arithmetic: 45.6 us -> none  [the longest x3 12.4 us: body(): lower_gram = jnp.linalg.cholesky(gram_sum + ridge_factor * identity)]
    all_gather x2 -> x0, blocking collectives: 27.2 us -> none  [the longest x1 22.1 us: body(): coef_rows = lax.all_gather(own_coef.T, ('gene', 'snp'), axis=0, tiled=True)]
    dot_general x5 -> x0, matrix products: 9.92 us -> none  [the longest x1 4.07 us: body(): jnp.dot(residual, dosage, preferred_element_type=jnp.float32) * norm_scale]
    all_to_all x1 -> x0, blocking collectives: 7.3 us -> none  [body(): lax.all_to_all(expression.T, 'samp', split_axis=0, concat_axis=1, tiled=T...]
    another operation x4 -> x0, matrix products: 3.01 us -> none  [the longest x2 1.6 us: body(): jax.scipy.linalg.cho_solve((lower_gram, True), factor_sum.T)]
  transfers between devices with their start and end apart: 3 -> 0, of which waited for: 2 -> 0; matrix products, arithmetic and copies ran while one was open for 13% -> 0% of each run, Pallas kernels for 0% -> 0%
where the time goes in v1:
time: 54 us; the launch traced here: 53.8 us
  Pallas kernels  53.8 us (100%)
    pallas_call x1, Pallas kernels, body(): pl.pallas_call(functools.partial(factor_kernel, (ns, ng, np_)), out_shape...  48 us
    pallas_call x1, Pallas kernels, body(): pl.pallas_call(functools.partial(assoc_kernel, 1.0 / samples ** 0.5), gri...  5.73 us

profile of v1, /device:TPU:0, one launch (start us, length us, event | category | flops | bytes accessed | tf_op | source)
XLA Modules:
  0.0 53.8 jit_solution(5016922994689309053)
XLA Ops:
  0.0 48.0 %factor_exchange.1 = (bf16[16,64,512]{2,1,0:T(8,128)(2,1)}, bf16[512,128]{1,0:T(8,128)(2,1)}, bf16[512,256]{1,0:T(8,128)(2,1)}) custom-call(bf16[256,128]{1,0:T(8,128)(2,1)} %expr_ref.1, bf16[128,128]{1,0:T(8,128)(2,1)} %load_ref.1), custom_call_target="tpu_custom_call" | custom-call | tf_op jit(solution)/shard_map/factor_exchange/pallas_call | solution.py:252
  48.0 5.7 %association.1 = bf16[1024,1024]{1,0:T(8,128)(2,1)} custom-call(bf16[1024,512]{1,0:T(8,128)(2,1)} %bitcast.4, bf16[512,256]{1,0:T(8,128)(2,1)} %get-tuple-element.9.proj_ref, bf16[512,128]{1,0:T(8,128)(2,1)} %get-tuple-element.10.fac_ref, bf16[512,1024]{1,0:T(8,128)(2,1)} %dosage_ref.1), custom_call_target="tpu_custom_call" | custom-call | tf_op jit(solution)/shard_map/association/pallas_call | solution.py:278
